TPU v7x, 768 devices: a whole 4x8x12 slice. The times are simulated.
768 devices in a mesh: member: 48 (over y_lo, z, core), domain: 16 (over x, y_hi).
Axes of the slice: x: 4, y: 8 (y_hi: 4, y_lo: 2; y = y_hi * 2 + y_lo), z: 12, core: 2. Of those that a mesh axis runs over, the one named last changes fastest.
Arguments:
- perturb: bfloat16 [192, 1536, 2048], P('member', None, 'domain'), may hold values from -20 to 20
- courant: float32 [2, 1536, 2048], P(None, 'member', 'domain'), may hold values from -0.45 to 0.45
- land_sea: int32 [1536, 2048], P('member', 'domain'), may hold values from 0 to 1, as said below
- basin_labels: int32 [96], replicated, may hold values from 0 to 3
- row_depth: float32 [1536], replicated, may hold values from 50 to 5000
- sample_column: int32 [3, 1536, 256], P(None, 'member', 'domain'), may hold values from 0 to 2047, as said below
- innovation: float32 [3, 1536, 256], P(None, 'member', 'domain'), may hold values from -6 to 6
- error_weight: float32 [3, 1536, 256], P(None, 'member', 'domain'), may hold values from 0.25 to 4
Outputs:
- increment: float32 [1536, 2048], P('member', 'domain')
- equivalents: float32 [3, 1536, 256], P(None, 'member', 'domain')
Inputs may be any that keep to these rules, and one draw needn't show every extreme that they name: `land_sea`: 0 marks land and 1 sea; rows 0 and 1535 are land. `sample_column`: entry j of a row lies in domain tile j // 16: 128 * (j // 16) <= value < 128 * (j // 16 + 1); columns may repeat.
All inputs are finite; a program needn't handle non-finite values.
Results may differ from a plain program's by a relative error of at most 0.0047.
Values may be sent and summed in bfloat16 or wider, within the bound.
A program may use at most 64 MiB of HBM per device.

v0:
```python
import jax
import jax.numpy as jnp
from jax import lax
from jax.sharding import PartitionSpec as P

NSTEP = 3
ITERS = 2
LOC_ROWS = 16


def padded_2(cells, sides, width):
    for axis, dim in sides:
        count = lax.axis_size(axis)
        head = lax.slice_in_dim(cells, 0, width, axis=dim)
        tail = lax.slice_in_dim(cells, cells.shape[dim] - width, cells.shape[dim], axis=dim)
        cells = jnp.concatenate(
            [
                lax.ppermute(tail, axis, [(i, (i + 1) % count) for i in range(count)]),
                cells,
                lax.ppermute(head, axis, [((i + 1) % count, i) for i in range(count)]),
            ],
            axis=dim,
        )
    return cells


def localization(basin_labels, row_depth, total_rows):
    row_index = jnp.arange(total_rows, dtype=jnp.int32)
    spacing = jnp.abs(row_index[:, None] - row_index[None, :])
    distance = jnp.minimum(spacing, total_rows - spacing).astype(jnp.float32)
    kernel = jnp.cosh(2.0 - 4.0 * distance / total_rows) / jnp.cosh(jnp.float32(2.0))
    labels = jnp.repeat(basin_labels, LOC_ROWS)
    matched = (labels[:, None] == labels[None, :]).astype(jnp.float32)
    log_depth = jnp.log(row_depth)
    depth_factor = jnp.exp(-jnp.abs(log_depth[:, None] - log_depth[None, :]))
    return (kernel * (1.0 + matched) * depth_factor).astype(jnp.bfloat16)


def tile_rim(state_field):
    return padded_2(state_field, (("member", 0), ("domain", 1)), 1)


def curvature_sum(partial_sum):
    return lax.psum(partial_sum, ("member", "domain"))


def misfit_sum(partial_sum):
    return lax.psum(partial_sum, ("member", "domain"))


def iterate(adjoint, tangent, covariance, own_rows, innovation, error_weight, field_shape):
    increment = jnp.zeros(field_shape, jnp.float32)
    control = jnp.zeros(field_shape, jnp.float32)
    equivalents = jnp.zeros(innovation.shape, jnp.float32)
    for iteration in range(ITERS):
        forcing = error_weight * (equivalents - innovation)
        adjoint_grad = adjoint(forcing)
        gradient = control + adjoint_grad
        direction = increment + covariance(adjoint_grad)
        own_curvature = jnp.sum(own_rows(gradient * direction, 0))
        curvature = curvature_sum(own_curvature)
        observed = tangent(direction)
        misfit = misfit_sum(jnp.sum(own_rows(error_weight * observed * observed, 1)))
        step_size = curvature / (curvature + misfit)
        increment = increment - step_size * direction
        control = control - step_size * gradient
        equivalents = equivalents - step_size * observed
    return (increment, equivalents)


def tiles_solve(perturb, courant, land_sea, sample_column, innovation, error_weight, localizer):
    members, total_rows, tile_width = perturb.shape
    slab_rows = land_sea.shape[0]
    ensemble = members * lax.axis_size("member")
    sea_mask = land_sea.astype(jnp.float32)
    neighbours = padded_2(courant, (("member", 1), ("domain", 2)), 1)
    eastward = jnp.maximum(courant[0], 0.0)
    westward = jnp.maximum(-courant[0], 0.0)
    northward = jnp.maximum(courant[1], 0.0)
    southward = jnp.maximum(-courant[1], 0.0)
    retain = 1.0 - jnp.abs(courant[0]) - jnp.abs(courant[1])
    east_near = jnp.maximum(neighbours[0], 0.0)
    west_near = jnp.maximum(-neighbours[0], 0.0)
    north_near = jnp.maximum(neighbours[1], 0.0)
    south_near = jnp.maximum(-neighbours[1], 0.0)
    first_col = lax.axis_index("domain") * tile_width
    positions = lax.broadcasted_iota(jnp.int32, (1, 1, 1, tile_width), 3) + first_col
    sample_picks = (sample_column[:, :, :, None] == positions).astype(jnp.float32)

    def advance(state_field):
        padded = tile_rim(state_field)
        advected = retain * state_field + eastward * padded[1:-1, :-2] + westward * padded[1:-1, 2:]
        advected = advected + northward * padded[:-2, 1:-1] + southward * padded[2:, 1:-1]
        return sea_mask * advected

    def retreat(adjoint_field):
        masked = sea_mask * adjoint_field
        padded = tile_rim(masked)
        result = (
            retain * masked
            + east_near[1:-1, 2:] * padded[1:-1, 2:]
            + west_near[1:-1, :-2] * padded[1:-1, :-2]
        )
        result = (
            result
            + north_near[2:, 1:-1] * padded[2:, 1:-1]
            + south_near[:-2, 1:-1] * padded[:-2, 1:-1]
        )
        return result

    def tangent(vector):
        state_field = vector
        observed = []
        for moment in range(NSTEP):
            state_field = advance(state_field)
            observed.append(jnp.sum(sample_picks[moment] * state_field[:, None, :], axis=2))
        return jnp.stack(observed)

    def adjoint(forcing):
        state_field = jnp.zeros((slab_rows, tile_width), jnp.float32)
        for moment in reversed(range(NSTEP)):
            state_field = state_field + jnp.sum(
                sample_picks[moment] * forcing[moment][:, :, None], axis=1
            )
            state_field = retreat(state_field)
        return state_field

    def covariance(vector):
        shared = (sea_mask * vector).astype(jnp.bfloat16)
        whole = lax.all_gather(shared, "member", axis=0, tiled=True)
        weighted = (perturb.astype(jnp.float32) * whole.astype(jnp.float32)[None]).astype(
            jnp.bfloat16
        )
        spread = jnp.einsum("ry,myx->mrx", localizer, weighted, preferred_element_type=jnp.float32)
        own_slice = perturb.astype(jnp.float32)
        summed = lax.psum_scatter(
            jnp.sum(own_slice * spread, axis=0), "member", scatter_dimension=0, tiled=True
        )
        return sea_mask * summed / (ensemble - 1)

    def own_rows(quantity, row_dim):
        return quantity

    return iterate(
        adjoint, tangent, covariance, own_rows, innovation, error_weight, (slab_rows, tile_width)
    )


def per_device(
    perturb, courant, land_sea, basin_labels, row_depth, sample_column, innovation, error_weight
):
    total_rows = perturb.shape[1]
    localizer = localization(basin_labels, row_depth, total_rows)
    return tiles_solve(
        perturb, courant, land_sea, sample_column, innovation, error_weight, localizer
    )


def solution(mesh):
    in_specs = (
        P("member", None, "domain"),
        P(None, "member", "domain"),
        P("member", "domain"),
        P(),
        P(),
        P(None, "member", "domain"),
        P(None, "member", "domain"),
        P(None, "member", "domain"),
    )
    out_specs = (P("member", "domain"), P(None, "member", "domain"))
    return jax.shard_map(
        per_device, mesh=mesh, in_specs=in_specs, out_specs=out_specs, check_vma=False
    )
```

profile of v0, /device:TPU:1, one launch (start us, length us, event | category | flops | bytes accessed | tf_op | source)
XLA Modules:
  0.0 977.9 jit_solution(13989570842975026495)
XLA Ops:
  10.4 12.4 %collective-permute-start.5 = (f32[1,128]{1,0:T(1,128)S(1)}, f32[1,128]{1,0:T(1,128)S(1)}, u32[]{:S(2)}, u32[]{:S(2)}) collective-permute-start(f32[1,128]{1,0:T(1,128)S(1)} %get-tuple-element.92), channel_id=1, source_target_pairs={{16,0},{32,16},{48,32},{64,48},{80,64},{96,80},{112,96},{128,112},... | collective-permute-start | bytes 1544 | tf_op jit(solution)/shard_map/ppermute | solution.py:20
  22.8 1.9 collective-permute-start.4
  24.8 1.9 collective-permute-start
  26.7 6.0 collective-permute-start.1
  33.6 4.2 collective-permute-start.2
  37.8 5.3 collective-permute-start.3
  43.1 3.9 collective-permute-start.6
  47.0 2.3 collective-permute-start.7
  49.5 6.3 collective-permute-done.7
  55.9 8.2 collective-permute-start.9
  64.2 1.9 collective-permute-start.8
  66.1 2.3 collective-permute-done.8
  68.5 1.9 collective-permute-start.10
  70.4 4.3 collective-permute-start.11
  74.7 4.6 collective-permute-done.11
  79.4 7.5 collective-permute-start.13
  86.9 1.9 collective-permute-start.12
  90.0 1.9 collective-permute-start.14
  91.9 4.3 collective-permute-start.15
  97.8 2.9 collective-permute-done.15
  100.8 50.9 %all_gather.6 = bf16[1536,128]{1,0:T(8,128)(2,1)S(1)} all-gather(bf16[32,128]{1,0:T(8,128)(2,1)S(1)} %get-tuple-element.28), channel_id=1, replica_groups=mesh['member'=48,'domain'=16] {'member'}, dimensions={0}, use_global_device_ids=true | all-gather | bytes 401408 | tf_op jit(solution)/shard_map/all_gather | solution.py:130
  152.7 11.9 %fusion.16 = f32[1536,128]{0,1:T(8,128)S(1)} fusion(bf16[4,1536,128]{1,2,0:T(8,128)(2,1)S(1)} %copy-done.3, f32[1536]{0:T(1024)S(1)} %log.3, s32[1536]{0:T(1024)S(1)} %eq.31, f32[1536,128]{0,1:T(8,128)} %copy.73), kind=kOutput, calls=%fused_computation.16 | convolution fusion | flops 2467627008 | bytes 3158016 | tf_op jit(solution)/shard_map/ry,myx->mrx/dot_general | solution.py:134
  165.8 159.5 %reduce-scatter.7.cloned.1.call-done = f32[32,128]{1,0:T(8,128)} async-done(((f32[1536,128]{1,0:T(8,128)}), f32[32,128]{1,0:T(8,128)}) %reduce-scatter.7.cloned.1.call-update) | async-done | bytes 16400 | tf_op jit(solution)/shard_map/reduce_scatter | solution.py:136
  326.6 3.5 collective-permute-start.16
  330.2 4.7 collective-permute-start.17
  335.7 4.0 collective-permute-start.18
  339.8 5.5 collective-permute-start.19
  346.2 2.5 collective-permute-start.20
  348.7 6.8 collective-permute-start.21
  356.4 4.9 collective-permute-start.22
  361.3 5.1 collective-permute-start.23
  367.5 1.9 collective-permute-start.24
  369.4 7.1 collective-permute-start.25
  377.4 2.8 collective-permute-start.26
  380.2 7.3 collective-permute-start.27
  389.3 114.6 %all-reduce.1 = (f32[]{:T(128)}, f32[]{:T(128)}) all-reduce(f32[]{:T(128)} %get-tuple-element.26, f32[]{:T(128)} %fusion.27), channel_id=1, replica_groups=mesh['member'=48,'domain'=16] {'member','domain'}, use_global_device_ids=true, to_apply=%region_6.0 | all-reduce | flops 2 | bytes 16 | tf_op jit(solution)/shard_map/psum | solution.py:44
  506.3 2.6 collective-permute-start.29
  508.8 3.0 collective-permute-start.28
  514.5 4.3 collective-permute-start.31
  518.8 4.5 collective-permute-done.31
  523.4 6.4 collective-permute-start.33
  529.8 1.9 collective-permute-start.32
  534.8 4.3 collective-permute-start.35
  539.1 4.5 collective-permute-done.35
  543.7 7.0 collective-permute-start.37
  550.7 2.1 collective-permute-start.36
  555.9 4.3 collective-permute-start.39
  560.2 4.5 collective-permute-done.39
  564.7 50.9 %all_gather.7 = bf16[1536,128]{1,0:T(8,128)(2,1)S(1)} all-gather(bf16[32,128]{1,0:T(8,128)(2,1)S(1)} %get-tuple-element.24), channel_id=1, replica_groups=mesh['member'=48,'domain'=16] {'member'}, dimensions={0}, use_global_device_ids=true | all-gather | bytes 401408 | tf_op jit(solution)/shard_map/all_gather | solution.py:130
  616.7 11.9 %fusion.18 = f32[1536,128]{0,1:T(8,128)S(1)} fusion(bf16[4,1536,128]{1,2,0:T(8,128)(2,1)S(1)} %copy-done.3, f32[1536]{0:T(1024)S(1)} %log.3, s32[1536]{0:T(1024)S(1)} %eq.31, f32[1536,128]{0,1:T(8,128)} %copy.78), kind=kOutput, calls=%fused_computation.18 | convolution fusion | flops 2467627008 | bytes 3158016 | tf_op jit(solution)/shard_map/ry,myx->mrx/dot_general | solution.py:134
  629.8 159.2 %reduce-scatter.9.cloned.1.call-done = f32[32,128]{1,0:T(8,128)} async-done(((f32[1536,128]{1,0:T(8,128)}), f32[32,128]{1,0:T(8,128)}) %reduce-scatter.9.cloned.1.call-update) | async-done | bytes 16400 | tf_op jit(solution)/shard_map/reduce_scatter | solution.py:136
  790.3 3.5 collective-permute-start.40
  793.8 4.7 collective-permute-start.41
  799.4 4.0 collective-permute-start.42
  803.4 5.5 collective-permute-start.43
  809.9 2.5 collective-permute-start.44
  812.4 6.8 collective-permute-start.45
  820.1 4.9 collective-permute-start.46
  825.0 5.3 collective-permute-start.47
  831.3 1.9 collective-permute-start.48
  833.3 7.1 collective-permute-start.49
  841.2 2.6 collective-permute-start.50
  843.8 7.5 collective-permute-start.51
  853.2 114.6 %all-reduce = (f32[]{:T(128)}, f32[]{:T(128)}) all-reduce(f32[]{:T(128)} %get-tuple-element.22, f32[]{:T(128)} %fusion.28), channel_id=1, replica_groups=mesh['member'=48,'domain'=16] {'member','domain'}, use_global_device_ids=true, to_apply=%region_18.0 | all-reduce | flops 2 | bytes 16 | tf_op jit(solution)/shard_map/psum | solution.py:44
  (149 shorter events, 38.0 us)
Async XLA Ops:
  7.2 3.2 copy-start
  7.2 17.6 %copy-start.1 = (f32[2,32,128]{2,1,0:T(8,128)S(1)}, f32[2,32,128]{2,1,0:T(8,128)}, u32[]{:S(2)}) copy-start(f32[2,32,128]{2,1,0:T(8,128)} %param.9) | copy-start | bytes 98308
  7.2 318.1 %reduce-scatter.7.cloned.1.call-start = ((), (), s32[]{:S(2)}) async-start(), calls=%async_computation.2 | async-start | bytes 802816 | tf_op jit(solution)/shard_map/reduce_scatter | solution.py:136
  9.7 79.1 %copy-start.5 = (f32[1536]{0:T(1024)S(1)}, f32[1536]{0:T(1024)}, u32[]{:S(2)}) copy-start(f32[1536]{0:T(1024)} %param.12) | copy-start | bytes 18436
  9.7 79.1 %copy-start.6 = (s32[96]{0:T(128)S(1)}, s32[96]{0:T(128)}, u32[]{:S(2)}) copy-start(s32[96]{0:T(128)} %param.11) | copy-start | bytes 1156
  9.7 86.4 %copy-start.2 = (bf16[4,1536,128]{2,1,0:T(8,128)(2,1)S(1)}, bf16[4,1536,128]{2,1,0:T(8,128)(2,1)}, u32[]{:S(2)}) copy-start(bf16[4,1536,128]{2,1,0:T(8,128)(2,1)} %param.8) | copy-start | bytes 4718596
  10.4 22.3 %collective-permute-start.5 = (f32[1,128]{1,0:T(1,128)S(1)}, f32[1,128]{1,0:T(1,128)S(1)}, u32[]{:S(2)}, u32[]{:S(2)}) collective-permute-start(f32[1,128]{1,0:T(1,128)S(1)} %get-tuple-element.92), channel_id=1, source_target_pairs={{16,0},{32,16},{48,32},{64,48},{80,64},{96,80},{112,96},{128,112},... | collective-permute-start | bytes 1544 | tf_op jit(solution)/shard_map/ppermute | solution.py:20
  22.8 9.9 %collective-permute-start.4 = (f32[1,128]{1,0:T(1,128)S(1)}, f32[1,128]{1,0:T(1,128)S(1)}, u32[]{:S(2)}, u32[]{:S(2)}) collective-permute-start(f32[1,128]{1,0:T(1,128)S(1)} %get-tuple-element.93), channel_id=1, source_target_pairs={{0,16},{16,32},{32,48},{48,64},{64,80},{80,96},{96,112},{112,128},... | collective-permute-start | bytes 1544 | tf_op jit(solution)/shard_map/ppermute | solution.py:18
  24.8 8.1 collective-permute-start
  26.7 6.8 collective-permute-start.1
  33.6 15.7 %collective-permute-start.2 = (f32[2,34,1]{2,1,0:T(8,128)S(1)}, f32[2,34,1]{2,1,0:T(8,128)S(1)}, u32[]{:S(2)}, u32[]{:S(2)}) collective-permute-start(f32[2,34,1]{2,1,0:T(8,128)S(1)} %get-tuple-element.42), channel_id=1, source_target_pairs={{0,1},{1,2},{2,3},{3,4},{4,5},{5,6},{6,7},{7,8},{8,9},{9,10},{10,1... | collective-permute-start | bytes 824 | tf_op jit(solution)/shard_map/ppermute | solution.py:18
  37.8 11.5 %collective-permute-start.3 = (f32[2,34,1]{2,1,0:T(8,128)S(1)}, f32[2,34,1]{2,1,0:T(8,128)S(1)}, u32[]{:S(2)}, u32[]{:S(2)}) collective-permute-start(f32[2,34,1]{2,1,0:T(8,128)S(1)} %get-tuple-element.43), channel_id=1, source_target_pairs={{1,0},{2,1},{3,2},{4,3},{5,4},{6,5},{7,6},{8,7},{9,8},{10,9},{11,1... | collective-permute-start | bytes 824 | tf_op jit(solution)/shard_map/ppermute | solution.py:20
  43.1 6.4 collective-permute-start.6
  47.0 8.8 collective-permute-start.7
  55.9 10.2 %collective-permute-start.9 = (f32[1,128]{1,0:T(1,128)S(1)}, f32[1,128]{1,0:T(1,128)S(1)}, u32[]{:S(2)}, u32[]{:S(2)}) collective-permute-start(f32[1,128]{1,0:T(1,128)S(1)} %get-tuple-element.90), channel_id=1, source_target_pairs={{16,0},{32,16},{48,32},{64,48},{80,64},{96,80},{112,96},{128,112},... | collective-permute-start | bytes 1544 | tf_op jit(solution)/shard_map/ppermute | solution.py:20
  64.2 4.2 collective-permute-start.8
  68.5 6.2 collective-permute-start.10
  70.4 8.8 collective-permute-start.11
  79.4 9.7 collective-permute-start.13
  86.9 3.0 collective-permute-start.12
  90.0 7.8 collective-permute-start.14
  91.9 8.8 collective-permute-start.15
  97.8 54.9 %copy-start.3 = (bf16[4,1536,128]{1,2,0:T(8,128)(2,1)S(1)}, bf16[4,1536,128]{1,2,0:T(8,128)(2,1)}, u32[]{:S(2)}) copy-start(bf16[4,1536,128]{1,2,0:T(8,128)(2,1)} %copy.69) | copy-start | bytes 4718596
  165.7 623.2 %reduce-scatter.9.cloned.1.call-start = ((), (), s32[]{:S(2)}) async-start(), calls=%async_computation.3 | async-start | bytes 802816 | tf_op jit(solution)/shard_map/reduce_scatter | solution.py:136
  326.6 8.2 collective-permute-start.16
  330.2 5.5 collective-permute-start.17
  335.7 9.5 collective-permute-start.18
  339.8 6.4 collective-permute-start.19
  346.2 9.3 collective-permute-start.20
  348.7 7.6 collective-permute-start.21
  356.4 10.1 %collective-permute-start.22 = (f32[34,1]{1,0:T(8,128)S(1)}, f32[34,1]{1,0:T(8,128)S(1)}, u32[]{:S(2)}, u32[]{:S(2)}) collective-permute-start(f32[34,1]{1,0:T(8,128)S(1)} %get-tuple-element.60), channel_id=1, source_target_pairs={{0,1},{1,2},{2,3},{3,4},{4,5},{5,6},{6,7},{7,8},{8,9},{9,10},{10,1... | collective-permute-start | bytes 416 | tf_op jit(solution)/shard_map/ppermute | solution.py:18
  361.3 6.0 collective-permute-start.23
  367.5 9.0 collective-permute-start.24
  369.4 7.9 collective-permute-start.25
  377.4 10.1 %collective-permute-start.26 = (f32[34,1]{1,0:T(8,128)S(1)}, f32[34,1]{1,0:T(8,128)S(1)}, u32[]{:S(2)}, u32[]{:S(2)}) collective-permute-start(f32[34,1]{1,0:T(8,128)S(1)} %get-tuple-element.58), channel_id=1, source_target_pairs={{0,1},{1,2},{2,3},{3,4},{4,5},{5,6},{6,7},{7,8},{8,9},{9,10},{10,1... | collective-permute-start | bytes 416 | tf_op jit(solution)/shard_map/ppermute | solution.py:18
  380.2 8.1 collective-permute-start.27
  506.3 5.6 collective-permute-start.29
  508.8 3.7 collective-permute-start.28
  512.6 6.2 collective-permute-start.30
  514.5 8.7 collective-permute-start.31
  523.4 8.3 collective-permute-start.33
  529.8 3.0 collective-permute-start.32
  532.9 6.2 collective-permute-start.34
  534.8 8.8 collective-permute-start.35
  543.7 9.1 collective-permute-start.37
  550.7 3.2 collective-permute-start.36
  554.0 6.2 collective-permute-start.38
  555.9 8.7 collective-permute-start.39
  628.6 160.4 %copy-start.4 = (f32[32,128]{1,0:T(8,128)S(1)}, f32[32,128]{1,0:T(8,128)}, u32[]{:S(2)}) copy-start(f32[32,128]{1,0:T(8,128)} %reduce-scatter.7.cloned.1.call-done) | copy-start | bytes 49156
  790.3 8.2 collective-permute-start.40
  793.8 5.5 collective-permute-start.41
  799.4 9.5 collective-permute-start.42
  803.4 6.4 collective-permute-start.43
  809.9 9.3 collective-permute-start.44
  812.4 7.6 collective-permute-start.45
  820.1 10.2 %collective-permute-start.46 = (f32[34,1]{1,0:T(8,128)S(1)}, f32[34,1]{1,0:T(8,128)S(1)}, u32[]{:S(2)}, u32[]{:S(2)}) collective-permute-start(f32[34,1]{1,0:T(8,128)S(1)} %get-tuple-element.48), channel_id=1, source_target_pairs={{0,1},{1,2},{2,3},{3,4},{4,5},{5,6},{6,7},{7,8},{8,9},{9,10},{10,1... | collective-permute-start | bytes 416 | tf_op jit(solution)/shard_map/ppermute | solution.py:18
  825.0 6.2 collective-permute-start.47
  831.3 9.0 collective-permute-start.48
  833.3 7.9 collective-permute-start.49
  841.2 10.1 %collective-permute-start.50 = (f32[34,1]{1,0:T(8,128)S(1)}, f32[34,1]{1,0:T(8,128)S(1)}, u32[]{:S(2)}, u32[]{:S(2)}) collective-permute-start(f32[34,1]{1,0:T(8,128)S(1)} %get-tuple-element.46), channel_id=1, source_target_pairs={{0,1},{1,2},{2,3},{3,4},{4,5},{5,6},{6,7},{7,8},{8,9},{9,10},{10,1... | collective-permute-start | bytes 416 | tf_op jit(solution)/shard_map/ppermute | solution.py:18
  843.8 8.4 collective-permute-start.51
Sparse Core Ops, SparseCore 0:
  165.9 159.3 reduce-scatter.6
  629.9 159.0 reduce-scatter.8
where the time goes:
time: 980 us; the launch traced here: 978 us
  waiting for transfers between devices  363 us (37%)
  blocking collectives  331 us (34%)
  starting transfers between devices  224 us (23%)
  matrix products  23.7 us (2%)
  between operations  19 us (2%)
  local copies, waits for them, and re-layouts  10.4 us (1%)
    reduce_scatter x2, waiting for transfers between devices, covariance(): lax.psum_scatter(jnp.sum(own_slice * spread, axis=0), 'member', scatter_d...  319 us
    psum x2, blocking collectives, curvature_sum(): return lax.psum(partial_sum, ('member', 'domain'))  229 us
    ppermute x26, starting transfers between devices, padded_2(): lax.ppermute(head, axis, [((i + 1) % count, i) for i in range(count)])  142 us
    all_gather x2, blocking collectives, covariance(): whole = lax.all_gather(shared, 'member', axis=0, tiled=True)  102 us
    ppermute x26, starting transfers between devices, padded_2(): lax.ppermute(tail, axis, [(i, (i + 1) % count) for i in range(count)])  81.6 us
    ppermute x26, waiting for transfers between devices, padded_2(): lax.ppermute(tail, axis, [(i, (i + 1) % count) for i in range(count)])  33.3 us
    dot_general x2, matrix products, covariance(): jnp.einsum('ry,myx->mrx', localizer, weighted, preferred_element_type=jnp...  23.7 us
  transfers between devices with their start and end apart: 54, of which 26 were waited for; matrix products, arithmetic and copies ran while one was open for 0% of the time, Pallas kernels for 0%

commit v1 on v0

v1 whole, which is shorter than its diff:
```python
import functools
import math

import jax
import jax.numpy as jnp
from jax import lax
from jax.experimental import pallas as pl
from jax.experimental.pallas import tpu as pltpu
from jax.sharding import PartitionSpec as P

NSTEP = 3
LOC_ROWS = 16
FIELDS = 9
EDGE = 8
SCALE = 2.0**-10
MESH = pl.DeviceIdType.MESH
F32 = jnp.float32
BF16 = jnp.bfloat16
AROUND = [(dm, dd) for dm in (-1, 0, 1) for dd in (-1, 0, 1) if (dm, dd) != (0, 0)]


def kernel(
    ensemble,
    pert_hbm,
    courant,
    land_sea,
    label_scalars,
    label_vector,
    depth_row,
    sample_column,
    innovation,
    error_weight,
    increment_out,
    equivalents_out,
    pert,
    loc,
    weighted,
    spread,
    base,
    depth_col,
    fields,
    pack_out,
    pack_in,
    coef,
    weight_ext,
    force_ext,
    whole,
    rs_send,
    rs_recv,
    grad,
    tile,
    seen,
    col_pad,
    ar_send,
    ar_a,
    ar_b,
    local_sem,
    pert_sems,
    rim_send,
    rim_recv,
    gat_send,
    gat_recv,
    fwd_send,
    fwd_recv,
    red_send,
    red_recv,
    ara_send,
    ara_recv,
    arb_send,
    arb_recv,
):
    count_m = lax.axis_size("member")
    count_d = lax.axis_size("domain")
    m = lax.axis_index("member")
    d = lax.axis_index("domain")
    peers = count_m // 2
    deep = peers // 2
    total = 32 * count_m
    tiles = total // 128
    core = lax.rem(m, 2)
    p = m // 2
    half = p // deep
    z = lax.rem(p, deep)
    sibling = {"member": 2 * p + 1 - core, "domain": d}

    def place_to(s):
        return lax.rem(half + lax.rem(s, 2), 2) * deep + lax.rem(z + s // 2, deep)

    def place_from(s):
        return lax.rem(half + lax.rem(s, 2), 2) * deep + lax.rem(z - s // 2 + deep, deep)

    def peer(s):
        return {"member": 2 * place_to(s) + core, "domain": d}

    def crossing(q):
        return {
            "member": 2 * p + lax.rem(core + lax.rem(q, 2), 2),
            "domain": lax.rem(d + q // 2, count_d),
        }

    def around(dm, dd):
        return {
            "member": lax.rem(m + dm + count_m, count_m),
            "domain": lax.rem(d + dd + count_d, count_d),
        }

    def remote(src, dst, send, recv, device):
        return pltpu.make_async_remote_copy(
            src_ref=src, dst_ref=dst, send_sem=send, recv_sem=recv, device_id=device, device_id_type=MESH
        )

    load = pltpu.make_async_copy(pert_hbm, pert.at[pl.ds(0, 4)], local_sem)
    load.start()

    barrier = pltpu.get_barrier_semaphore()

    def greet_peer(s, carry):
        pl.semaphore_signal(barrier, inc=1, device_id=peer(s), device_id_type=MESH)
        return carry

    def greet_crossing(q, carry):
        pl.semaphore_signal(barrier, inc=1, device_id=crossing(q), device_id_type=MESH)
        return carry

    for dm, dd in AROUND:
        pl.semaphore_signal(barrier, inc=1, device_id=around(dm, dd), device_id_type=MESH)
    lax.fori_loop(1, peers, greet_peer, 0)
    lax.fori_loop(1, 2 * count_d, greet_crossing, 0)

    lane = lax.broadcasted_iota(jnp.int32, (32, 128), 1)
    sea = land_sea[...].astype(F32)
    fields[0, 0:32, :] = courant[0]
    fields[1, 0:32, :] = courant[1]
    fields[2, 0:32, :] = sea
    for t in range(NSTEP):
        column = sample_column[t] - d * 128
        col_pad[t] = jnp.zeros((32, 128), jnp.int32)
        col_pad[t, :, 0:16] = column
        ew = error_weight[t]
        push = -ew * innovation[t]
        w_sum = jnp.zeros((32, 128), F32)
        g_sum = jnp.zeros((32, 128), F32)
        for j in range(16):
            hit = column[:, j : j + 1] == lane
            w_sum = w_sum + jnp.where(hit, ew[:, j : j + 1], 0.0)
            g_sum = g_sum + jnp.where(hit, push[:, j : j + 1], 0.0)
        fields[3 + t, 0:32, :] = w_sum
        fields[6 + t, 0:32, :] = g_sum
    first = jnp.zeros((32, 128), F32)
    last = jnp.zeros((32, 128), F32)
    for f in range(FIELDS):
        here = (lane >= EDGE * f) & (lane < EDGE * (f + 1))
        value = fields[f, 0:32, :]
        turned = value if f == 0 else pltpu.roll(value, EDGE * f, 1)
        first = jnp.where(here, turned, first)
        last = jnp.where(here, pltpu.roll(value, EDGE * (f + 1), 1), last)
    pack_out[0] = first
    pack_out[1] = last

    pl.semaphore_wait(barrier, 8 + (peers - 1) + (2 * count_d - 1))

    def rows_of(dm):
        if dm == 0:
            return slice(0, 32), slice(0, 32)
        if dm == 1:
            return slice(24, 32), slice(40, 48)
        return slice(0, 8), slice(32, 40)

    def rim_copy(n, i):
        dm, dd = AROUND[i]
        src, dst = rows_of(dm)
        if n == 0:
            if dd == 0:
                a, b = fields.at[:, src, :], fields.at[:, dst, :]
            else:
                side = 0 if dd < 0 else 1
                a, b = pack_out.at[side, src, :], pack_in.at[side, dst, :]
        else:
            a = tile.at[n - 1, 0, src, :]
            b = tile.at[n - 1, 0 if dd == 0 else (1 if dd < 0 else 2), dst, :]
        return remote(a, b, rim_send.at[n, i], rim_recv.at[n, i], around(dm, dd))

    for i in range(8):
        rim_copy(0, i).start()
    share = remote(pert_hbm, pert.at[pl.ds(4, 4)], pert_sems.at[0], pert_sems.at[1], sibling)
    share.start()

    row_i = lax.broadcasted_iota(jnp.int32, (128, 128), 0)
    lane_i = lax.broadcasted_iota(jnp.int32, (128, 128), 1)
    for t in range(tiles):
        gap = jnp.abs(lane_i + 128 * t - row_i)
        gap = jnp.minimum(gap, total - gap).astype(F32)
        x = 2.0 - 4.0 * gap / total
        value = (jnp.exp(x) + jnp.exp(-x)) / (2.0 * math.cosh(2.0))
        base[:, 128 * t : 128 * (t + 1)] = value
        base[:, total + 128 * t : total + 128 * (t + 1)] = value
        row = jnp.broadcast_to(depth_row[:, 128 * t : 128 * (t + 1)], (128, 128))
        turned = row.T
        depth_col[0, 128 * t : 128 * (t + 1), :] = turned
        depth_col[1, 128 * t : 128 * (t + 1), :] = 1.0 / turned
    blocks = total // LOC_ROWS
    spot = lax.broadcasted_iota(jnp.int32, (blocks, total), 1) // LOC_ROWS
    own_block = lax.broadcasted_iota(jnp.int32, (blocks, total), 0)
    labels = jnp.dot(
        jnp.broadcast_to(label_vector[...].astype(F32), (8, blocks)),
        (spot == own_block).astype(F32),
        preferred_element_type=F32,
    )[0:1, :]
    depth = depth_row[...]
    depth_inv = 1.0 / depth

    def localize(s, carry):
        q = place_to(s)
        for h in range(2):
            label = label_scalars[4 * q + 2 * core + h].astype(F32)
            factor = jnp.where(jnp.abs(labels - label) < 0.5, 2.0, 1.0)
            near = depth * factor
            near_inv = depth_inv * factor
            rows = pl.ds(pl.multiple_of(64 * q + 32 * core + 16 * h, 16), 16)
            base_rows = pl.ds(pl.multiple_of(64 * lax.rem(q, 2) + 32 * core + 16 * h, 16), 16)
            a = depth_col[0, rows, :]
            a_inv = depth_col[1, rows, :]
            out_rows = pl.ds(pl.multiple_of(32 * s + 16 * h, 16), 16)
            for t in range(tiles):
                cols = slice(128 * t, 128 * (t + 1))
                ratio = jnp.minimum(a * near_inv[:, cols], a_inv * near[:, cols])
                offset = pl.multiple_of(128 * (tiles - q // 2 + t), 128)
                loc[out_rows, cols] = (ratio * base[base_rows, pl.ds(offset, 128)]).astype(BF16)
        return carry

    split = peers // 2
    lax.fori_loop(0, split, localize, 0)

    for i in range(8):
        rim_copy(0, i).wait()

    lane48 = lax.broadcasted_iota(jnp.int32, (48, 128), 1)
    ext = []
    for f in range(FIELDS):
        right = pack_in[0] if f == 0 else pltpu.roll(pack_in[0], 128 - EDGE * f, 1)
        left = pltpu.roll(pack_in[1], 128 - EDGE * (f + 1), 1)
        ext.append(jnp.concatenate([fields[f], jnp.where(lane48 < 64, right, left)], axis=1))
    cu, cv, sea_ext = ext[0], ext[1], ext[2]
    coef[0] = 1.0 - jnp.abs(cu) - jnp.abs(cv)
    coef[1] = jnp.maximum(cu, 0.0)
    coef[2] = jnp.maximum(-cu, 0.0)
    coef[3] = jnp.maximum(cv, 0.0)
    coef[4] = jnp.maximum(-cv, 0.0)
    coef[5] = sea_ext
    for t in range(NSTEP):
        weight_ext[t] = ext[3 + t]
        force_ext[t] = ext[6 + t]

    def shift(value, by, axis):
        return pltpu.roll(value, by % value.shape[axis], axis)

    def advance(s):
        moved = coef[0] * s + coef[1] * shift(s, 1, 1) + coef[2] * shift(s, -1, 1)
        moved = moved + coef[3] * shift(s, 1, 0) + coef[4] * shift(s, -1, 0)
        return coef[5] * moved

    def retreat(adj):
        masked = coef[5] * adj
        back = coef[0] * masked + shift(coef[1] * masked, -1, 1) + shift(coef[2] * masked, 1, 1)
        return back + shift(coef[3] * masked, -1, 0) + shift(coef[4] * masked, 1, 0)

    def adjoint(forces):
        adj = retreat(forces[2])
        adj = retreat(adj + forces[1])
        return retreat(adj + forces[0])[0:32, 0:128]

    def scatter_gather(n):
        whole[n, p, core] = (sea * grad[n]).astype(BF16)

        def gather_copy(s, where):
            return remote(
                whole.at[n, where, core],
                whole.at[n, where, core],
                gat_send.at[n, s],
                gat_recv.at[n, s],
                peer(s),
            )

        def forward_copy(s, side):
            q = place_from(s)
            return remote(
                whole.at[n, q, side], whole.at[n, q, side], fwd_send.at[n, s], fwd_recv.at[n, s], sibling
            )

        def send(s, carry):
            gather_copy(s, p).start()
            return carry

        forward_copy(0, core).start()
        lax.fori_loop(1, peers, send, 0)
        if n == 0:
            lax.fori_loop(split, peers, localize, 0)
            load.wait()
            share.wait()

        def weigh(q, side):
            rows = pl.ds(pl.multiple_of(64 * q + 32 * side, 32), 32)
            v = whole[n, q, side]
            for k in range(8):
                weighted[rows, 128 * k : 128 * (k + 1)] = pert[k, rows, :] * v

        def arrive(s, carry):
            gather_copy(s, place_from(s)).wait_recv()
            forward_copy(s, core).start()
            weigh(place_from(s), core)
            return carry

        def arrive_forward(s, carry):
            forward_copy(s, 1 - core).wait_recv()
            weigh(place_from(s), 1 - core)
            return carry

        weigh(p, core)
        lax.fori_loop(1, peers, arrive, 0)
        lax.fori_loop(0, peers, arrive_forward, 0)

        def reduce_copy(s):
            return remote(
                rs_send.at[n, s], rs_recv.at[n, s], red_send.at[n, s], red_recv.at[n, s], peer(s)
            )

        chunks = 3 if peers % 3 == 0 else 2
        slots = peers // chunks

        def share_of(s, i):
            rows = pl.ds(pl.multiple_of(64 * place_to(s) + 32 * core, 32), 32)
            rows_in = pl.ds(pl.multiple_of(32 * i, 32), 32)
            acc = pert[0, rows, :].astype(F32) * spread[rows_in, 0:128]
            for k in range(1, 8):
                acc = acc + pert[k, rows, :].astype(F32) * spread[rows_in, 128 * k : 128 * (k + 1)]
            return acc

        def chunk(step, carry):
            ci = lax.rem(step + 1, chunks)
            first_row = pl.multiple_of(ci * slots * 32, 32)
            spread[...] = jnp.dot(
                loc[pl.ds(first_row, slots * 32), :], weighted[...], preferred_element_type=F32
            )

            def out(i, inner):
                s = ci * slots + i

                @pl.when(s > 0)
                def _():
                    rs_send[n, s] = share_of(s, i).astype(BF16)
                    reduce_copy(s).start()

                return inner

            lax.fori_loop(0, slots, out, 0)
            return carry

        lax.fori_loop(0, chunks, chunk, 0)
        acc = share_of(0, 0)

        def collect(s, acc):
            reduce_copy(s).wait_recv()
            return acc + rs_recv[n, s].astype(F32)

        acc = lax.fori_loop(1, peers, collect, acc)
        tile[n, 0, 0:32, :] = sea * acc / (ensemble - 1)
        for i in range(8):
            rim_copy(n + 1, i).start()

    def finish_sends(n):
        def body(s, carry):
            remote(
                whole.at[n, p, core], whole.at[n, p, core], gat_send.at[n, s], gat_recv.at[n, s], peer(s)
            ).wait_send()
            remote(
                rs_send.at[n, s], rs_recv.at[n, s], red_send.at[n, s], red_recv.at[n, s], peer(s)
            ).wait_send()
            return carry

        def body_forward(s, carry):
            q = place_from(s)
            remote(
                whole.at[n, q, core], whole.at[n, q, core], fwd_send.at[n, s], fwd_recv.at[n, s], sibling
            ).wait_send()
            return carry

        lax.fori_loop(1, peers, body, 0)
        lax.fori_loop(0, peers, body_forward, 0)

    def widened(n):
        for i in range(8):
            rim_copy(n + 1, i).wait()
        side = jnp.where(lane48 < 64, tile[n, 1], tile[n, 2])
        return jnp.concatenate([tile[n, 0], side], axis=1)

    def tangent(s):
        states = []
        for t in range(NSTEP):
            s = advance(s)
            states.append(s)
        return states

    def sample(states, n):
        for t in range(NSTEP):
            seen[n, t] = jnp.take_along_axis(states[t][0:32, 0:128], col_pad[t], axis=1)

    def added(value):
        return jnp.sum(jnp.sum(value, axis=0, keepdims=True), axis=1, keepdims=True)

    def inner(x):
        return x[0:32, 0:128]

    grad[0] = adjoint([force_ext[t] for t in range(NSTEP)])
    scatter_gather(0)
    first_states = tangent(widened(0))
    pulls = [weight_ext[t] * first_states[t] for t in range(NSTEP)]
    grad[1] = adjoint(pulls) * SCALE
    for t in range(NSTEP):
        force_ext[t] = pulls[t]
    first_own = first_states
    sample(first_states, 0)
    misfit_11 = added(sum(inner(pulls[t]) * inner(first_own[t]) for t in range(NSTEP)))
    scatter_gather(1)
    finish_sends(0)
    d1 = tile[0, 0, 0:32, :]
    d2 = tile[1, 0, 0:32, :]
    curve_11 = added(grad[0] * d1)
    curve_12 = added(grad[0] * d2 + grad[1] * d1)
    curve_22 = added(grad[1] * d2)
    second_states = tangent(widened(1))
    misfit_12 = added(sum(inner(force_ext[t]) * inner(second_states[t]) for t in range(NSTEP)))
    misfit_22 = added(
        sum(inner(weight_ext[t]) * inner(second_states[t]) * inner(second_states[t]) for t in range(NSTEP))
    )

    lane1 = lax.broadcasted_iota(jnp.int32, (1, 128), 1)
    sums = jnp.zeros((1, 128), F32)
    for i, value in enumerate((curve_11, curve_12, curve_22, misfit_11, misfit_12, misfit_22)):
        sums = jnp.where(lane1 == i, value, sums)

    def ar_copy(stage, s):
        if stage == 0:
            return remote(ar_send.at[0], ar_a.at[s], ara_send.at[s], ara_recv.at[s], peer(s))
        return remote(ar_send.at[1], ar_b.at[s], arb_send.at[s], arb_recv.at[s], crossing(s))

    for stage, slots in ((0, peers), (1, 2 * count_d)):
        ar_send[stage] = sums

        def start(s, carry):
            ar_copy(stage, s).start()
            return carry

        def gain(s, acc):
            ar_copy(stage, s).wait_recv()
            return acc + (ar_a[s] if stage == 0 else ar_b[s])

        lax.fori_loop(1, slots, start, 0)
        if stage == 0:
            sample(second_states, 1)
            finish_sends(1)
        sums = lax.fori_loop(1, slots, gain, sums)

    def total_of(i):
        return jnp.sum(jnp.where(lane1 == i, sums, 0.0), axis=1, keepdims=True)

    curve_11, curve_12, curve_22 = total_of(0), total_of(1), total_of(2)
    misfit_11, misfit_12, misfit_22 = total_of(3), total_of(4), total_of(5)
    step_1 = curve_11 / (curve_11 + misfit_11)
    keep = 1.0 - step_1
    mix = step_1 * (1.0 / SCALE)
    curve = keep * keep * curve_11 - mix * keep * curve_12 + mix * mix * curve_22
    misfit = keep * keep * misfit_11 - 2.0 * mix * keep * misfit_12 + mix * mix * misfit_22
    step_2 = curve / (curve + misfit)
    a = -step_1 - step_2 * keep
    b = step_2 * mix
    increment_out[...] = a * d1 + b * d2
    for t in range(NSTEP):
        equivalents_out[t] = (a * seen[0, t] + b * seen[1, t])[:, 0:16]

    def end(stage):
        def body(s, carry):
            ar_copy(stage, s).wait_send()
            return carry

        return body

    lax.fori_loop(1, peers, end(0), 0)
    lax.fori_loop(1, 2 * count_d, end(1), 0)


def per_device(
    perturb, courant, land_sea, basin_labels, row_depth, sample_column, innovation, error_weight
):
    members, total, width = perturb.shape
    rows = land_sea.shape[0]
    count_m = lax.axis_size("member")
    count_d = lax.axis_size("domain")
    peers = count_m // 2
    chunks = 3 if peers % 3 == 0 else 2
    vmem = pl.BlockSpec(memory_space=pltpu.VMEM)
    dma = pltpu.SemaphoreType.DMA
    return pl.pallas_call(
        functools.partial(kernel, members * count_m),
        out_shape=(
            jax.ShapeDtypeStruct((rows, width), F32),
            jax.ShapeDtypeStruct(innovation.shape, F32),
        ),
        in_specs=[
            pl.BlockSpec(memory_space=pl.ANY),
            vmem,
            vmem,
            pl.BlockSpec(memory_space=pltpu.SMEM),
            vmem,
            vmem,
            vmem,
            vmem,
            vmem,
        ],
        out_specs=(vmem, vmem),
        scratch_shapes=[
            pltpu.VMEM((2 * members, total, width), BF16),
            pltpu.VMEM((total // 2, total), BF16),
            pltpu.VMEM((total, 2 * members * width), BF16),
            pltpu.VMEM((total // 2 // chunks, 2 * members * width), F32),
            pltpu.VMEM((128, 2 * total), F32),
            pltpu.VMEM((2, total, 128), F32),
            pltpu.VMEM((FIELDS, 48, 128), F32),
            pltpu.VMEM((2, 32, 128), F32),
            pltpu.VMEM((2, 48, 128), F32),
            pltpu.VMEM((6, 48, 256), F32),
            pltpu.VMEM((NSTEP, 48, 256), F32),
            pltpu.VMEM((NSTEP, 48, 256), F32),
            pltpu.VMEM((2, peers, 2, 32, 128), BF16),
            pltpu.VMEM((2, peers, 32, 128), BF16),
            pltpu.VMEM((2, peers, 32, 128), BF16),
            pltpu.VMEM((2, 32, 128), F32),
            pltpu.VMEM((2, 3, 48, 128), F32),
            pltpu.VMEM((2, NSTEP, 32, 128), F32),
            pltpu.VMEM((NSTEP, 32, 128), jnp.int32),
            pltpu.VMEM((2, 1, 128), F32),
            pltpu.VMEM((peers, 1, 128), F32),
            pltpu.VMEM((2 * count_d, 1, 128), F32),
            dma,
            dma((2,)),
            dma((3, 8)),
            dma((3, 8)),
            dma((2, peers)),
            dma((2, peers)),
            dma((2, peers)),
            dma((2, peers)),
            dma((2, peers)),
            dma((2, peers)),
            dma((peers,)),
            dma((peers,)),
            dma((2 * count_d,)),
            dma((2 * count_d,)),
        ],
        compiler_params=pltpu.CompilerParams(
            collective_id=0, has_side_effects=True, vmem_limit_bytes=48 * 1024 * 1024
        ),
    )(
        perturb,
        courant,
        land_sea,
        basin_labels,
        basin_labels.reshape(1, -1),
        row_depth.reshape(1, -1),
        sample_column,
        innovation,
        error_weight,
    )


def solution(mesh):
    in_specs = (
        P("member", None, "domain"),
        P(None, "member", "domain"),
        P("member", "domain"),
        P(),
        P(),
        P(None, "member", "domain"),
        P(None, "member", "domain"),
        P(None, "member", "domain"),
    )
    out_specs = (P("member", "domain"), P(None, "member", "domain"))
    return jax.shard_map(
        per_device, mesh=mesh, in_specs=in_specs, out_specs=out_specs, check_vma=False
    )
```

time: 980 us -> 109 us (0.11)
  waiting for transfers between devices: 363 us -> 0 us
  blocking collectives: 331 us -> 0 us
  starting transfers between devices: 224 us -> 0 us
  Pallas kernels: 0 us -> 100 us
  matrix products: 23.7 us -> 0 us
  between operations: 19 us -> 0.65 us
    reduce_scatter x2 -> x0, waiting for transfers between devices: 319 us -> none  [covariance(): lax.psum_scatter(jnp.sum(own_slice * spread, axis=0), 'member', scatter_d...]
    psum x2 -> x0, blocking collectives: 229 us -> none  [curvature_sum(): return lax.psum(partial_sum, ('member', 'domain'))]
    ppermute x52 -> x0, starting transfers between devices: 224 us -> none  [the longest x26 142 us: padded_2(): lax.ppermute(head, axis, [((i + 1) % count, i) for i in range(count)])]
    all_gather x2 -> x0, blocking collectives: 102 us -> none  [covariance(): whole = lax.all_gather(shared, 'member', axis=0, tiled=True)]
    pallas_call x0 -> x1, Pallas kernels: none -> 100 us  [per_device(): pl.pallas_call(functools.partial(kernel, members * count_m), out_shape=(j...]
    ppermute x52 -> x0, waiting for transfers between devices: 44 us -> none  [the longest x26 33.3 us: padded_2(): lax.ppermute(tail, axis, [(i, (i + 1) % count) for i in range(count)])]
    dot_general x2 -> x0, matrix products: 23.7 us -> none  [covariance(): jnp.einsum('ry,myx->mrx', localizer, weighted, preferred_element_type=jnp...]
  transfers between devices with their start and end apart: 54 -> 0, of which waited for: 26 -> 0; matrix products, arithmetic and copies ran while one was open for 0% -> 0% of each run, Pallas kernels for 0% -> 0%
where the time goes in v1:
time: 109 us
  Pallas kernels  100 us (92%)
  local copies, waits for them, and re-layouts  7.98 us (7%)
    pallas_call x1, Pallas kernels, per_device(): pl.pallas_call(functools.partial(kernel, members * count_m), out_shape=(j...  100 us
    unnamed x12, local copies, waits for them, and re-layouts  6.59 us

profile of v1, /device:TPU:1, one launch (start us, length us, event | category | flops | bytes accessed | tf_op | source)
XLA Modules:
  0.0 108.7 jit_solution(2741768662124904896)
XLA Ops:
  0.6 0.7 reshape.11.depth_row
  1.3 0.8 copy.10.sample_column
  2.1 0.8 copy.11.innovation
  3.0 0.8 copy.12.error_weight
  3.8 0.0 copy-start
  3.8 1.4 %copy-done = bf16[4,1536,128]{2,1,0:T(8,128)(2,1)S(1)} copy-done((bf16[4,1536,128]{2,1,0:T(8,128)(2,1)S(1)}, bf16[4,1536,128]{2,1,0:T(8,128)(2,1)}, u32[]{:S(2)}) %copy-start) | copy-done | bytes 1572888
  5.2 0.0 copy-start.1
  5.2 0.8 copy-done.1
  6.0 0.0 copy-start.2
  6.0 0.7 copy-done.2
  6.7 0.0 copy-start.3
  6.7 0.7 copy-done.3
  7.3 100.0 %shard_map.95 = (f32[32,128]{1,0:T(8,128)S(1)}, f32[3,32,16]{2,1,0:T(8,128)S(1)}) custom-call(bf16[4,1536,128]{2,1,0:T(8,128)(2,1)S(1)} %copy-done, f32[2,32,128]{2,1,0:T(8,128)S(1)} %copy-done.1, s32[32,128]{1,0:T(8,128)S(1)} %copy-done.2, s32[96]{0:T(128)S(1)} %copy-done.3, s32[1,96]{1,0:T(1,128)S(1)} %bitcast.1, f32[1,1536]{1,0:T(1,128)S(1)} %reshape.11.depth_row, ...), custom_call_target="tpu_custom_call" | custom-call | tf_op jit(solution)/shard_map/pallas_call | solution.py:502
  107.4 0.7 copy.13
  108.1 0.6 copy.15
Async XLA Ops:
  3.8 1.4 %copy-start = (bf16[4,1536,128]{2,1,0:T(8,128)(2,1)S(1)}, bf16[4,1536,128]{2,1,0:T(8,128)(2,1)}, u32[]{:S(2)}) copy-start(bf16[4,1536,128]{2,1,0:T(8,128)(2,1)} %pert_hbm.1) | copy-start | bytes 4718596
  5.2 0.8 copy-start.1
  6.0 0.7 copy-start.2
  6.7 0.7 copy-start.3

commit v2 on v1

v2 whole, which is shorter than its diff:
```python
import functools
import math

import jax
import jax.numpy as jnp
from jax import lax
from jax.experimental import pallas as pl
from jax.experimental.pallas import tpu as pltpu
from jax.sharding import PartitionSpec as P

NSTEP = 3
LOC_ROWS = 16
FIELDS = 9
CHUNKS = 4
EDGE = 8
SCALE = 2.0**-10
MESH = pl.DeviceIdType.MESH
F32 = jnp.float32
BF16 = jnp.bfloat16
AROUND = [(dm, dd) for dm in (-1, 0, 1) for dd in (-1, 0, 1) if (dm, dd) != (0, 0)]


def kernel(
    ensemble,
    pert_hbm,
    courant_hbm,
    sea_hbm,
    label_hbm,
    depth_hbm,
    column_hbm,
    innovation_hbm,
    weight_hbm,
    increment_out,
    equivalents_out,
    pert,
    loc,
    weighted,
    spread,
    base,
    depth_col,
    depth_row,
    label_scalars,
    label_vector,
    land_sea,
    obs_int,
    obs_real,
    turn,
    fields,
    pack_out,
    pack_in,
    coef,
    weight_ext,
    force_ext,
    whole,
    rs_send,
    rs_recv,
    grad,
    tile,
    seen,
    pick,
    ar_send,
    ar_a,
    ar_b,
    local_sems,
    pert_sems,
    rim_send,
    rim_recv,
    gat_send,
    gat_recv,
    fwd_recv,
    red_send,
    red_recv,
    ar_send_sem,
    ar_recv_sem,
):
    count_m = lax.axis_size("member")
    count_d = lax.axis_size("domain")
    m = lax.axis_index("member")
    d = lax.axis_index("domain")
    peers = count_m // 2
    deep = peers // 2
    total = 32 * count_m
    tiles = total // 128
    core = lax.rem(m, 2)
    p = m // 2
    half = p // deep
    z = lax.rem(p, deep)
    sibling = {"member": 2 * p + 1 - core, "domain": d}

    near = min(2, deep // 6)
    low, high = near + 1, deep - near
    third = (high - low) // 3
    groups = [(low + third, high - third), (low, low + third), (high - third, high)]
    groups = [group for group in groups if group[0] < group[1]]

    def plane(dy):
        return lax.rem(half + dy, 2)

    def ahead(dz):
        return lax.rem(z + dz, deep)

    def member(plane_at, z_at, core_at):
        return {"member": 2 * (plane_at * deep + z_at) + core_at, "domain": d}

    def other(core_step):
        return lax.rem(core + core_step, 2)

    def slot_place(s):
        k = s // 2
        dz = deep // 2 + (1 - 2 * lax.rem(k, 2)) * ((k + 1) // 2)
        return plane(1 - lax.rem(s, 2)), ahead(dz)

    def place_to(s):
        plane_at, z_at = slot_place(s)
        return plane_at * deep + z_at

    def peer(s):
        return {"member": 2 * place_to(s) + core, "domain": d}

    def crossing(q):
        return {
            "member": 2 * p + lax.rem(core + lax.rem(q, 2), 2),
            "domain": lax.rem(d + q // 2, count_d),
        }

    def around(dm, dd):
        return {
            "member": lax.rem(m + dm + count_m, count_m),
            "domain": lax.rem(d + dd + count_d, count_d),
        }

    def remote(src, dst, send, recv, device):
        return pltpu.make_async_remote_copy(
            src_ref=src, dst_ref=dst, send_sem=send, recv_sem=recv, device_id=device, device_id_type=MESH
        )

    loads = [
        pltpu.make_async_copy(source, target, local_sems.at[i])
        for i, (source, target) in enumerate(
            (
                (column_hbm, obs_int),
                (innovation_hbm, obs_real.at[0]),
                (weight_hbm, obs_real.at[1]),
                (sea_hbm, land_sea),
                (courant_hbm, fields.at[0:2, 0:32, :]),
                (depth_hbm, depth_row),
                (label_hbm, label_scalars),
                (label_hbm, label_vector),
                (pert_hbm, pert.at[pl.ds(0, 4)]),
            )
        )
    ]
    for copy in loads:
        copy.start()

    barrier = pltpu.get_barrier_semaphore()

    def greet_member(j, carry):
        device = {"member": lax.rem(m + j, count_m), "domain": d}
        pl.semaphore_signal(barrier, inc=1, device_id=device, device_id_type=MESH)
        return carry

    def greet_crossing(q, carry):
        pl.semaphore_signal(barrier, inc=1, device_id=crossing(q), device_id_type=MESH)
        return carry

    for dm, dd in AROUND:
        pl.semaphore_signal(barrier, inc=1, device_id=around(dm, dd), device_id_type=MESH)
    lax.fori_loop(1, count_m, greet_member, 0)
    lax.fori_loop(1, 2 * count_d, greet_crossing, 0)

    lane = lax.broadcasted_iota(jnp.int32, (32, 128), 1)
    for copy in loads[:5]:
        copy.wait()
    sea = land_sea[...].astype(F32)
    fields[2, 0:32, :] = sea
    turn[...] = jnp.zeros((2, 128, 128), F32)
    for t in range(NSTEP):
        turn[0, 16 * t : 16 * t + 16, 0:32] = (obs_int[t] - d * 128).astype(F32)
        turn[0, 48 + 16 * t : 64 + 16 * t, 0:32] = obs_real[1, t]
        turn[1, 16 * t : 16 * t + 16, 0:32] = -obs_real[1, t] * obs_real[0, t]
    across = turn[0].T[0:32, :]
    push = turn[1].T[0:32, :]
    column = across.astype(jnp.int32)
    pick[...] = column
    for t in range(NSTEP):
        w_sum = jnp.zeros((32, 128), F32)
        g_sum = jnp.zeros((32, 128), F32)
        for j in range(16 * t, 16 * t + 16):
            hit = column[:, j : j + 1] == lane
            w_sum = w_sum + jnp.where(hit, across[:, 48 + j : 49 + j], 0.0)
            g_sum = g_sum + jnp.where(hit, push[:, j : j + 1], 0.0)
        fields[3 + t, 0:32, :] = w_sum
        fields[6 + t, 0:32, :] = g_sum
    first = jnp.zeros((32, 128), F32)
    last = jnp.zeros((32, 128), F32)
    for f in range(FIELDS):
        here = (lane >= EDGE * f) & (lane < EDGE * (f + 1))
        value = fields[f, 0:32, :]
        turned = value if f == 0 else pltpu.roll(value, EDGE * f, 1)
        first = jnp.where(here, turned, first)
        last = jnp.where(here, pltpu.roll(value, EDGE * (f + 1), 1), last)
    pack_out[0] = first
    pack_out[1] = last

    pl.semaphore_wait(barrier, 8 + (count_m - 1) + (2 * count_d - 1))

    def rows_of(dm):
        if dm == 0:
            return slice(0, 32), slice(0, 32)
        if dm == 1:
            return slice(24, 32), slice(40, 48)
        return slice(0, 8), slice(32, 40)

    def rim_copy(n, i):
        dm, dd = AROUND[i]
        src, dst = rows_of(dm)
        sem = 0
        if n == 0:
            if dd == 0:
                a, b = fields.at[:, src, :], fields.at[:, dst, :]
            else:
                side, sem = (0 if dd < 0 else 1), 1
                a, b = pack_out.at[side, src, :], pack_in.at[side, dst, :]
        else:
            at = 0 if dd == 0 else (48 if dd < 0 else 96)
            a = tile.at[n - 1, src, :]
            b = tile.at[n - 1, slice(dst.start + at, dst.stop + at), :]
        return remote(a, b, rim_send.at[n, sem], rim_recv.at[n, sem], around(dm, dd))

    def rim_wait(n):
        def both(ref, sem):
            copy = remote(ref, ref, rim_send.at[n, sem], rim_recv.at[n, sem], sibling)
            copy.wait_recv()
            copy.wait_send()

        if n == 0:
            both(fields.at[:, 32:48, :], 0)
            both(pack_in, 1)
        else:
            both(tile.at[n - 1, 32:144, :], 0)

    for i in range(8):
        rim_copy(0, i).start()
    share = remote(pert_hbm, pert.at[pl.ds(4, 4)], pert_sems.at[0], pert_sems.at[1], sibling)
    share.start()

    for copy in loads[5:8]:
        copy.wait()

    row_i = lax.broadcasted_iota(jnp.int32, (128, 128), 0)
    lane_i = lax.broadcasted_iota(jnp.int32, (128, 128), 1)
    for t in range(tiles):
        gap = jnp.abs(lane_i + 128 * t - row_i)
        gap = jnp.minimum(gap, total - gap).astype(F32)
        x = 2.0 - 4.0 * gap / total
        value = (jnp.exp(x) + jnp.exp(-x)) / (2.0 * math.cosh(2.0))
        base[:, 128 * t : 128 * (t + 1)] = value
        base[:, total + 128 * t : total + 128 * (t + 1)] = value
        row = jnp.broadcast_to(depth_row[t : t + 1, :], (128, 128))
        turned = row.T
        depth_col[0, 128 * t : 128 * (t + 1), :] = turned
        depth_col[1, 128 * t : 128 * (t + 1), :] = 1.0 / turned
    blocks = total // LOC_ROWS
    spot = lax.broadcasted_iota(jnp.int32, (blocks, total), 1) // LOC_ROWS
    own_block = lax.broadcasted_iota(jnp.int32, (blocks, total), 0)
    labels = jnp.dot(
        jnp.broadcast_to(label_vector[...].astype(F32), (8, blocks)),
        (spot == own_block).astype(F32),
        preferred_element_type=F32,
    )[0:1, :]
    depth = jnp.concatenate([depth_row[t : t + 1, :] for t in range(tiles)], axis=1)
    depth_inv = 1.0 / depth

    def localize(s, carry):
        q = place_to(s)
        for h in range(2):
            label = label_scalars[0, 4 * q + 2 * core + h].astype(F32)
            factor = jnp.where(jnp.abs(labels - label) < 0.5, 2.0, 1.0)
            by = depth * factor
            by_inv = depth_inv * factor
            rows = pl.ds(pl.multiple_of(64 * q + 32 * core + 16 * h, 16), 16)
            base_rows = pl.ds(pl.multiple_of(64 * lax.rem(q, 2) + 32 * core + 16 * h, 16), 16)
            a = depth_col[0, rows, :]
            a_inv = depth_col[1, rows, :]
            out_rows = pl.ds(pl.multiple_of(32 * s + 16 * h, 16), 16)
            for t in range(tiles):
                cols = slice(128 * t, 128 * (t + 1))
                ratio = jnp.minimum(a * by_inv[:, cols], a_inv * by[:, cols])
                offset = pl.multiple_of(128 * (tiles - q // 2 + t), 128)
                loc[out_rows, cols] = (ratio * base[base_rows, pl.ds(offset, 128)]).astype(BF16)
        return carry

    split = peers // 2
    lax.fori_loop(0, split, localize, 0)

    rim_wait(0)

    lane48 = lax.broadcasted_iota(jnp.int32, (48, 128), 1)
    ext = []
    for f in range(FIELDS):
        right = pack_in[0] if f == 0 else pltpu.roll(pack_in[0], 128 - EDGE * f, 1)
        left = pltpu.roll(pack_in[1], 128 - EDGE * (f + 1), 1)
        ext.append(jnp.concatenate([fields[f], jnp.where(lane48 < 64, right, left)], axis=1))
    cu, cv, sea_ext = ext[0], ext[1], ext[2]
    coef[0] = 1.0 - jnp.abs(cu) - jnp.abs(cv)
    coef[1] = jnp.maximum(cu, 0.0)
    coef[2] = jnp.maximum(-cu, 0.0)
    coef[3] = jnp.maximum(cv, 0.0)
    coef[4] = jnp.maximum(-cv, 0.0)
    coef[5] = sea_ext
    for t in range(NSTEP):
        weight_ext[t] = ext[3 + t]
        force_ext[t] = ext[6 + t]

    def shift(value, by, axis):
        return pltpu.roll(value, by % value.shape[axis], axis)

    def advance(s):
        moved = coef[0] * s + coef[1] * shift(s, 1, 1) + coef[2] * shift(s, -1, 1)
        moved = moved + coef[3] * shift(s, 1, 0) + coef[4] * shift(s, -1, 0)
        return coef[5] * moved

    def retreat(adj):
        masked = coef[5] * adj
        back = coef[0] * masked + shift(coef[1] * masked, -1, 1) + shift(coef[2] * masked, 1, 1)
        return back + shift(coef[3] * masked, -1, 0) + shift(coef[4] * masked, 1, 0)

    def adjoint(forces):
        adj = retreat(forces[2])
        adj = retreat(adj + forces[1])
        return retreat(adj + forces[0])[0:32, 0:128]

    def slot(dy, dc, dz):
        return (2 * dy + dc) * deep + dz

    combos = [(0, 1), (1, 0), (1, 1)]
    near_steps = sorted((k for k in range(deep) if not low <= k < high), key=lambda k: -min(k, deep - k))
    far_count, near_count = high - low, 4 * len(near_steps) - 1

    def gathered(n, start, count, send_sem, recv_sem):
        ref = whole.at[n, pl.ds(start, count)]
        return remote(ref, ref, send_sem, recv_sem, sibling)

    def scatter_gather(n, meanwhile):
        whole[n, 0] = (sea * grad[n]).astype(BF16)

        def send(dy, dc, dz, sem):
            remote(
                whole.at[n, 0],
                whole.at[n, slot(dy, dc, dz)],
                gat_send.at[n, 0],
                gat_recv.at[n, sem],
                member(plane(dy), ahead(dz), other(dc)),
            ).start()

        for g, (start, stop) in enumerate(groups):
            for dz in range(start, stop):
                send(0, 0, dz, g)
        for dz in near_steps:
            for dy, dc in combos + [(0, 0)]:
                if (dy, dc, dz) != (0, 0, 0):
                    send(dy, dc, dz, 3)
        meanwhile()

        def weigh(dy, dc, start, stop):
            def body(dz, carry):
                q = plane(dy) * deep + ahead(deep - dz)
                rows = pl.ds(pl.multiple_of(64 * q + 32 * other(dc), 32), 32)
                v = whole[n, slot(dy, dc, dz)]
                for k in range(8):
                    weighted[rows, 128 * k : 128 * (k + 1)] = pert[k, rows, :] * v
                return carry

            lax.fori_loop(start, stop, body, 0)

        for g, (start, stop) in enumerate(groups):
            count = stop - start
            gathered(n, start, count, gat_send.at[n, 0], gat_recv.at[n, g]).wait_recv()
            for i, (dy, dc) in enumerate(combos):
                remote(
                    whole.at[n, pl.ds(start, count)],
                    whole.at[n, pl.ds(slot(dy, dc, start), count)],
                    gat_send.at[n, 1],
                    fwd_recv.at[n, 3 * g + i],
                    member(plane(dy), z, other(dc)),
                ).start()
        if far_count:
            weigh(0, 0, low, high)
        gathered(n, 0, near_count, gat_send.at[n, 0], gat_recv.at[n, 3]).wait_recv()
        for dy, dc in combos + [(0, 0)]:
            weigh(dy, dc, 0, low)
            if near:
                weigh(dy, dc, high, deep)
        for g, (start, stop) in enumerate(groups):
            for i, (dy, dc) in enumerate(combos):
                gathered(
                    n, slot(dy, dc, start), stop - start, gat_send.at[n, 1], fwd_recv.at[n, 3 * g + i]
                ).wait_recv()
                weigh(dy, dc, start, stop)

        def reduce_copy(s):
            return remote(rs_send.at[n, s], rs_recv.at[n, s], red_send.at[n], red_recv.at[n], peer(s))

        chunks = CHUNKS if peers % CHUNKS == 0 else 2
        slots = peers // chunks

        def share_of(s, i):
            rows = pl.ds(pl.multiple_of(64 * place_to(s) + 32 * core, 32), 32)
            rows_in = pl.ds(pl.multiple_of(32 * i, 32), 32)
            acc = pert[0, rows, :].astype(F32) * spread[rows_in, 0:128]
            for k in range(1, 8):
                acc = acc + pert[k, rows, :].astype(F32) * spread[rows_in, 128 * k : 128 * (k + 1)]
            return acc

        def chunk(ci, carry):
            first_row = pl.multiple_of(ci * slots * 32, 32)
            spread[...] = jnp.dot(
                loc[pl.ds(first_row, slots * 32), :], weighted[...], preferred_element_type=F32
            )

            def out(i, inner):
                s = ci * slots + i

                @pl.when(s < peers - 1)
                def _():
                    rs_send[n, s] = share_of(s, i).astype(BF16)
                    reduce_copy(s).start()

                return inner

            lax.fori_loop(0, slots, out, 0)
            return carry

        lax.fori_loop(0, chunks, chunk, 0)
        acc = share_of(peers - 1, slots - 1)
        remote(rs_send.at[n], rs_recv.at[n], red_send.at[n], red_recv.at[n], sibling).wait_recv()

        def collect(s, acc):
            return acc + rs_recv[n, s].astype(F32)

        acc = lax.fori_loop(0, peers - 1, collect, acc, unroll=True)
        tile[n, 0:32, :] = sea * acc / (ensemble - 1)
        for i in range(8):
            rim_copy(n + 1, i).start()

    def finish_sends(n):
        remote(rs_send.at[n], rs_recv.at[n], red_send.at[n], red_recv.at[n], sibling).wait_send()
        gathered(n, 0, far_count + near_count, gat_send.at[n, 0], gat_recv.at[n, 3]).wait_send()
        if far_count:
            gathered(n, 0, 3 * far_count, gat_send.at[n, 1], gat_recv.at[n, 3]).wait_send()

    def widened(n):
        rim_wait(n + 1)
        side = jnp.where(lane48 < 64, tile[n, 48:96, :], tile[n, 96:144, :])
        return jnp.concatenate([tile[n, 0:48, :], side], axis=1)

    def tangent(s):
        states = []
        for t in range(NSTEP):
            s = advance(s)
            states.append(s)
        return states

    def sample(states, n):
        got = jnp.zeros((32, 128), F32)
        for t in range(NSTEP):
            taken = jnp.take_along_axis(states[t][0:32, 0:128], pick[...], axis=1)
            got = jnp.where((lane >= 16 * t) & (lane < 16 * t + 16), taken, got)
        seen[n] = got

    def added(value):
        return jnp.sum(jnp.sum(value, axis=0, keepdims=True), axis=1, keepdims=True)

    def inner(x):
        return x[0:32, 0:128]

    grad[0] = adjoint([force_ext[t] for t in range(NSTEP)])

    def rest_of_setup():
        lax.fori_loop(split, peers, localize, 0)
        loads[8].wait()
        share.wait()

    scatter_gather(0, rest_of_setup)
    first_states = tangent(widened(0))
    pulls = [weight_ext[t] * first_states[t] for t in range(NSTEP)]
    grad[1] = adjoint(pulls) * SCALE
    results = []

    def rest_of_first():
        for t in range(NSTEP):
            force_ext[t] = pulls[t]
        sample(first_states, 0)
        results.append(added(sum(inner(pulls[t]) * inner(first_states[t]) for t in range(NSTEP))))

    scatter_gather(1, rest_of_first)
    misfit_11 = results[0]
    finish_sends(0)
    d1 = tile[0, 0:32, :]
    d2 = tile[1, 0:32, :]
    curve_11 = added(grad[0] * d1)
    curve_12 = added(grad[0] * d2 + grad[1] * d1)
    curve_22 = added(grad[1] * d2)
    second_states = tangent(widened(1))
    misfit_12 = added(sum(inner(force_ext[t]) * inner(second_states[t]) for t in range(NSTEP)))
    misfit_22 = added(
        sum(inner(weight_ext[t]) * inner(second_states[t]) * inner(second_states[t]) for t in range(NSTEP))
    )

    lane1 = lax.broadcasted_iota(jnp.int32, (1, 128), 1)
    sums = jnp.zeros((1, 128), F32)
    for i, value in enumerate((curve_11, curve_12, curve_22, misfit_11, misfit_12, misfit_22)):
        sums = jnp.where(lane1 == i, value, sums)

    def ar_refs(stage):
        return ar_a if stage == 0 else ar_b

    def ar_copy(stage, s):
        device = peer(s) if stage == 0 else crossing(s + 1)
        return remote(
            ar_send.at[stage], ar_refs(stage).at[s], ar_send_sem.at[stage], ar_recv_sem.at[stage], device
        )

    def ar_all(stage):
        ref = ar_refs(stage)
        return remote(ref, ref, ar_send_sem.at[stage], ar_recv_sem.at[stage], sibling)

    for stage, slots in ((0, peers - 1), (1, 2 * count_d - 1)):
        ar_send[stage] = sums

        def start(s, carry):
            ar_copy(stage, s).start()
            return carry

        lax.fori_loop(0, slots, start, 0)
        if stage == 0:
            sample(second_states, 1)
            finish_sends(1)
        ar_all(stage).wait_recv()
        sums = sums + jnp.sum(ar_refs(stage)[...], axis=0)

    def total_of(i):
        return jnp.sum(jnp.where(lane1 == i, sums, 0.0), axis=1, keepdims=True)

    curve_11, curve_12, curve_22 = total_of(0), total_of(1), total_of(2)
    misfit_11, misfit_12, misfit_22 = total_of(3), total_of(4), total_of(5)
    step_1 = curve_11 / (curve_11 + misfit_11)
    keep = 1.0 - step_1
    mix = step_1 * (1.0 / SCALE)
    curve = keep * keep * curve_11 - mix * keep * curve_12 + mix * mix * curve_22
    misfit = keep * keep * misfit_11 - 2.0 * mix * keep * misfit_12 + mix * mix * misfit_22
    step_2 = curve / (curve + misfit)
    a = -step_1 - step_2 * keep
    b = step_2 * mix
    increment_out[...] = a * d1 + b * d2
    turn[0, 0:32, :] = a * seen[0] + b * seen[1]
    down = turn[0].T
    for t in range(NSTEP):
        equivalents_out[t] = down[16 * t : 16 * t + 16, 0:32]
    ar_all(0).wait_send()
    ar_all(1).wait_send()


def per_device(
    perturb, courant, land_sea, basin_labels, row_depth, sample_column, innovation, error_weight
):
    members, total, width = perturb.shape
    rows = land_sea.shape[0]
    count_m = lax.axis_size("member")
    count_d = lax.axis_size("domain")
    peers = count_m // 2
    chunks = CHUNKS if peers % CHUNKS == 0 else 2
    vmem = pl.BlockSpec(memory_space=pltpu.VMEM)
    hbm = pl.BlockSpec(memory_space=pltpu.HBM)
    slots = innovation.shape[2]
    dma = pltpu.SemaphoreType.DMA
    increment, equivalents = pl.pallas_call(
        functools.partial(kernel, members * count_m),
        out_shape=(
            jax.ShapeDtypeStruct((rows, width), F32),
            jax.ShapeDtypeStruct((NSTEP, slots, rows), F32),
        ),
        in_specs=[hbm] * 8,
        out_specs=(vmem, vmem),
        scratch_shapes=[
            pltpu.VMEM((2 * members, total, width), BF16),
            pltpu.VMEM((total // 2, total), BF16),
            pltpu.VMEM((total, 2 * members * width), BF16),
            pltpu.VMEM((total // 2 // chunks, 2 * members * width), F32),
            pltpu.VMEM((128, 2 * total), F32),
            pltpu.VMEM((2, total, 128), F32),
            pltpu.VMEM((total // 128, 128), F32),
            pltpu.SMEM((1, basin_labels.shape[0]), jnp.int32),
            pltpu.VMEM((1, basin_labels.shape[0]), jnp.int32),
            pltpu.VMEM((rows, width), jnp.int32),
            pltpu.VMEM((NSTEP, slots, rows), jnp.int32),
            pltpu.VMEM((2, NSTEP, slots, rows), F32),
            pltpu.VMEM((2, 128, 128), F32),
            pltpu.VMEM((FIELDS, 48, 128), F32),
            pltpu.VMEM((2, 32, 128), F32),
            pltpu.VMEM((2, 48, 128), F32),
            pltpu.VMEM((6, 48, 256), F32),
            pltpu.VMEM((NSTEP, 48, 256), F32),
            pltpu.VMEM((NSTEP, 48, 256), F32),
            pltpu.VMEM((2, count_m, 32, 128), BF16),
            pltpu.VMEM((2, peers - 1, 32, 128), BF16),
            pltpu.VMEM((2, peers - 1, 32, 128), BF16),
            pltpu.VMEM((2, 32, 128), F32),
            pltpu.VMEM((2, 144, 128), F32),
            pltpu.VMEM((2, 32, 128), F32),
            pltpu.VMEM((32, 128), jnp.int32),
            pltpu.VMEM((2, 1, 128), F32),
            pltpu.VMEM((peers - 1, 1, 128), F32),
            pltpu.VMEM((2 * count_d - 1, 1, 128), F32),
            dma((9,)),
            dma((2,)),
            dma((3, 2)),
            dma((3, 2)),
            dma((2, 2)),
            dma((2, 4)),
            dma((2, 9)),
            dma((2,)),
            dma((2,)),
            dma((2,)),
            dma((2,)),
        ],
        compiler_params=pltpu.CompilerParams(
            collective_id=0, has_side_effects=True, vmem_limit_bytes=60 * 1024 * 1024
        ),
    )(
        perturb,
        courant,
        land_sea,
        basin_labels.reshape(1, -1),
        row_depth.reshape(-1, 128),
        jnp.transpose(sample_column, (0, 2, 1)),
        jnp.transpose(innovation, (0, 2, 1)),
        jnp.transpose(error_weight, (0, 2, 1)),
    )
    return increment, jnp.transpose(equivalents, (0, 2, 1))


def solution(mesh):
    in_specs = (
        P("member", None, "domain"),
        P(None, "member", "domain"),
        P("member", "domain"),
        P(),
        P(),
        P(None, "member", "domain"),
        P(None, "member", "domain"),
        P(None, "member", "domain"),
    )
    out_specs = (P("member", "domain"), P(None, "member", "domain"))
    return jax.shard_map(
        per_device, mesh=mesh, in_specs=in_specs, out_specs=out_specs, check_vma=False
    )
```

time: 109 us -> 95.2 us (0.87)
  Pallas kernels: 100 us -> 91.6 us
  local copies, waits for them, and re-layouts: 7.98 us -> 2.67 us
    pallas_call x1, Pallas kernels: 100 us -> 91.6 us  [per_device(): pl.pallas_call(functools.partial(kernel, members * count_m), out_shape=(j...]
    unnamed x12 -> x2, local copies, waits for them, and re-layouts: 6.59 us -> 2.67 us
where the time goes in v2:
time: 95.2 us; the launch traced here: 94.9 us
  Pallas kernels  91.6 us (96%)
  local copies, waits for them, and re-layouts  2.67 us (3%)
    pallas_call x1, Pallas kernels, per_device(): pl.pallas_call(functools.partial(kernel, members * count_m), out_shape=(j...  91.6 us
    unnamed x2, local copies, waits for them, and re-layouts  2.67 us

profile of v2, /device:TPU:1, one launch (start us, length us, event | category | flops | bytes accessed | tf_op | source)
XLA Modules:
  0.0 94.9 jit_solution(13585078894579494004)
XLA Ops:
  0.6 91.6 %shard_map.95 = (f32[32,128]{1,0:T(8,128)}, f32[3,16,32]{2,1,0:T(8,128)}) custom-call(bf16[4,1536,128]{2,1,0:T(8,128)(2,1)} %pert_hbm.1, f32[2,32,128]{2,1,0:T(8,128)} %courant_hbm.1, s32[32,128]{1,0:T(8,128)} %sea_hbm.1, s32[1,96]{1,0:T(1,128)} %bitcast.11, f32[12,128]{1,0:T(8,128)} %bitcast.10, s32[3,16,32]{2,1,0:T(8,128)} %bitcast.7, ...), custom_call_target="tpu_custom_call" | custom-call | tf_op jit(solution)/shard_map/pallas_call | solution.py:578
  92.2 1.3 %copy.12 = f32[32,128]{1,0:T(8,128)} copy(f32[32,128]{1,0:T(8,128)} %get-tuple-element.8) | data formatting | bytes 32768
  93.6 1.3 %copy.13 = f32[3,32,16]{1,2,0:T(8,128)} copy(f32[3,32,16]{1,2,0:T(8,128)} %bitcast.6) | data formatting | bytes 12288

commit v3 on v2

--- a/solution.py
+++ b/solution.py
@@ -17,7 +17,7 @@
 MESH = pl.DeviceIdType.MESH
 F32 = jnp.float32
 BF16 = jnp.bfloat16
-AROUND = [(dm, dd) for dm in (-1, 0, 1) for dd in (-1, 0, 1) if (dm, dd) != (0, 0)]
+AROUND = [(1, 1), (1, -1), (-1, 1), (-1, -1), (0, 1), (0, -1), (1, 0), (-1, 0)]
 
 
 def kernel(
@@ -88,7 +88,7 @@
     sibling = {"member": 2 * p + 1 - core, "domain": d}
 
     near = min(2, deep // 6)
-    low, high = near + 1, deep - near
+    low, high = max(near, 1), deep - near
     third = (high - low) // 3
     groups = [(low + third, high - third), (low, low + third), (high - third, high)]
     groups = [group for group in groups if group[0] < group[1]]
@@ -228,17 +228,18 @@
             b = tile.at[n - 1, slice(dst.start + at, dst.stop + at), :]
         return remote(a, b, rim_send.at[n, sem], rim_recv.at[n, sem], around(dm, dd))
 
+    def rim_parts(n):
+        if n == 0:
+            return ((fields.at[:, 32:48, :], 0), (pack_in, 1))
+        return ((tile.at[n - 1, 32:144, :], 0),)
+
     def rim_wait(n):
-        def both(ref, sem):
-            copy = remote(ref, ref, rim_send.at[n, sem], rim_recv.at[n, sem], sibling)
-            copy.wait_recv()
-            copy.wait_send()
-
-        if n == 0:
-            both(fields.at[:, 32:48, :], 0)
-            both(pack_in, 1)
-        else:
-            both(tile.at[n - 1, 32:144, :], 0)
+        for ref, sem in rim_parts(n):
+            remote(ref, ref, rim_send.at[n, sem], rim_recv.at[n, sem], sibling).wait_recv()
+
+    def rim_sent(n):
+        for ref, sem in rim_parts(n):
+            remote(ref, ref, rim_send.at[n, sem], rim_recv.at[n, sem], sibling).wait_send()
 
     for i in range(8):
         rim_copy(0, i).start()
@@ -467,7 +468,8 @@
         for t in range(NSTEP):
             taken = jnp.take_along_axis(states[t][0:32, 0:128], pick[...], axis=1)
             got = jnp.where((lane >= 16 * t) & (lane < 16 * t + 16), taken, got)
-        seen[n] = got
+        turn[n, 0:32, :] = got
+        seen[n] = turn[n].T[0:48, 0:32]
 
     def added(value):
         return jnp.sum(jnp.sum(value, axis=0, keepdims=True), axis=1, keepdims=True)
@@ -480,7 +482,7 @@
     def rest_of_setup():
         lax.fori_loop(split, peers, localize, 0)
         loads[8].wait()
-        share.wait()
+        share.wait_recv()
 
     scatter_gather(0, rest_of_setup)
     first_states = tangent(widened(0))
@@ -533,10 +535,12 @@
             ar_copy(stage, s).start()
             return carry
 
-        lax.fori_loop(0, slots, start, 0)
+        lax.fori_loop(0, slots, start, 0, unroll=True)
         if stage == 0:
             sample(second_states, 1)
             finish_sends(1)
+            for n in range(3):
+                rim_sent(n)
         ar_all(stage).wait_recv()
         sums = sums + jnp.sum(ar_refs(stage)[...], axis=0)
 
@@ -554,12 +558,17 @@
     a = -step_1 - step_2 * keep
     b = step_2 * mix
     increment_out[...] = a * d1 + b * d2
-    turn[0, 0:32, :] = a * seen[0] + b * seen[1]
-    down = turn[0].T
     for t in range(NSTEP):
-        equivalents_out[t] = down[16 * t : 16 * t + 16, 0:32]
+        own = slice(16 * t, 16 * t + 16)
+        equivalents_out[t] = a * seen[0, own, :] + b * seen[1, own, :]
+    share.wait_send()
     ar_all(0).wait_send()
     ar_all(1).wait_send()
+
+
+def settle(increment, equivalents, increment_out, equivalents_out):
+    increment_out[...] = increment[...]
+    equivalents_out[...] = equivalents[...]
 
 
 def per_device(
@@ -575,12 +584,13 @@
     hbm = pl.BlockSpec(memory_space=pltpu.HBM)
     slots = innovation.shape[2]
     dma = pltpu.SemaphoreType.DMA
-    increment, equivalents = pl.pallas_call(
+    shapes = (
+        jax.ShapeDtypeStruct((rows, width), F32),
+        jax.ShapeDtypeStruct((NSTEP, slots, rows), F32),
+    )
+    results = pl.pallas_call(
         functools.partial(kernel, members * count_m),
-        out_shape=(
-            jax.ShapeDtypeStruct((rows, width), F32),
-            jax.ShapeDtypeStruct((NSTEP, slots, rows), F32),
-        ),
+        out_shape=shapes,
         in_specs=[hbm] * 8,
         out_specs=(vmem, vmem),
         scratch_shapes=[
@@ -608,7 +618,7 @@
             pltpu.VMEM((2, peers - 1, 32, 128), BF16),
             pltpu.VMEM((2, 32, 128), F32),
             pltpu.VMEM((2, 144, 128), F32),
-            pltpu.VMEM((2, 32, 128), F32),
+            pltpu.VMEM((2, NSTEP * slots, rows), F32),
             pltpu.VMEM((32, 128), jnp.int32),
             pltpu.VMEM((2, 1, 128), F32),
             pltpu.VMEM((peers - 1, 1, 128), F32),
@@ -638,6 +648,13 @@
         jnp.transpose(innovation, (0, 2, 1)),
         jnp.transpose(error_weight, (0, 2, 1)),
     )
+    increment, equivalents = pl.pallas_call(
+        settle,
+        out_shape=shapes,
+        in_specs=[vmem, vmem],
+        out_specs=(vmem, vmem),
+        compiler_params=pltpu.CompilerParams(vmem_limit_bytes=60 * 1024 * 1024),
+    )(*results)
     return increment, jnp.transpose(equivalents, (0, 2, 1))
 
 

time: 95.2 us -> 95.1 us (level)
  local copies, waits for them, and re-layouts: 2.67 us -> 0 us
  Pallas kernels: 91.6 us -> 94.2 us
    unnamed x2 -> x0, local copies, waits for them, and re-layouts: 2.67 us -> none
    pallas_call x1 -> x2, Pallas kernels: 91.6 us -> 94.2 us  [the longest x1 92.8 us: per_device(): pl.pallas_call(functools.partial(kernel, members * count_m), out_shape=sh...]
where the time goes in v3:
time: 95.1 us; the launch traced here: 94.9 us
  Pallas kernels  94.2 us (99%)
    pallas_call x1, Pallas kernels, per_device(): pl.pallas_call(functools.partial(kernel, members * count_m), out_shape=sh...  92.8 us

profile of v3, /device:TPU:1, one launch (start us, length us, event | category | flops | bytes accessed | tf_op | source)
XLA Modules:
  0.0 94.9 jit_solution(3866288632749708052)
XLA Ops:
  0.6 92.8 %shard_map.95 = (f32[32,128]{1,0:T(8,128)}, f32[3,16,32]{2,1,0:T(8,128)}) custom-call(bf16[4,1536,128]{2,1,0:T(8,128)(2,1)} %pert_hbm.1, f32[2,32,128]{2,1,0:T(8,128)} %courant_hbm.1, s32[32,128]{1,0:T(8,128)} %sea_hbm.1, s32[1,96]{1,0:T(1,128)} %bitcast.10, f32[12,128]{1,0:T(8,128)} %bitcast.9, s32[3,16,32]{2,1,0:T(8,128)} %bitcast.6, ...), custom_call_target="tpu_custom_call" | custom-call | tf_op jit(solution)/shard_map/pallas_call | solution.py:591
  93.5 1.4 %shard_map.96 = (f32[32,128]{1,0:T(8,128)}, f32[3,16,32]{2,1,0:T(8,128)}) custom-call(f32[32,128]{1,0:T(8,128)} %get-tuple-element.6.increment, f32[3,16,32]{2,1,0:T(8,128)} %get-tuple-element.7.equivalents), custom_call_target="tpu_custom_call" | custom-call | tf_op jit(solution)/shard_map/pallas_call | solution.py:651
